TPU v7x, 32 devices: a whole 2x2x4 slice. The times are simulated.
32 devices in a mesh: groups: 2 (over y), vocab: 8 (over z, x), tok: 2 (over core).
Axes of the slice: x: 2, y: 2, z: 4, core: 2. Of those that a mesh axis runs over, the one named last changes fastest.
Arguments:
- hidden_rows: bfloat16 [512, 4096], P(('groups', 'vocab'), 'tok'), parts along dimension 0, may hold values from -4 to 4
- head_weight: bfloat16 [4096, 6144], P('tok', 'vocab'), may hold values from -4 to 4
- block_links: int32 [2, 64], P(None, 'vocab'), may hold values from -1 to 2, as said below
- teacher_rows: int32 [64, 128], P('vocab'), may hold values from 0 to 255, as said below
- offsets: int32 [64, 4, 128], P('vocab'), may hold values from 0 to 255, as said below
- link_weights: bfloat16 [64, 4, 128], P('vocab'), may hold values from 0.049804688 to 1
Outputs:
- log_partition: float32 [512], P(('groups', 'tok')), parts along dimension 0
- student_targets: float32 [512, 6144], P(('groups', 'tok'), 'vocab'), parts along dimension 0
There are 2 independent parts, one for each index of `groups`. A program takes and returns all parts, laid end to end along the dimension named above; an argument that names none is the same for every part. Nothing has to cross between parts.
Inputs may be any that keep to these rules, and one draw needn't show every extreme that they name: `block_links`: row 0 of a slot is a teacher block of its shard, 0 to 2; row 1 is a block of the owner's 3 student blocks, or -1 where the slot is padding. Every teacher block of every shard has a live slot. `teacher_rows`: the 128 entries of one slot are distinct entries of its teacher block; every teacher entry of every shard is used by some live slot. The 4 offsets of one used teacher entry of a slot are distinct.
All inputs are finite; a program needn't handle non-finite values.
Results may differ from a plain program's by a relative error of at most 0.0029.
Values may be sent and summed in bfloat16 or wider, within the bound.
A program may use at most 64 MiB of HBM per device.

v0:
```python
import math

import jax
import jax.numpy as jnp
from jax import lax
from jax.sharding import PartitionSpec as P

BLOCK = 256
SB_DEV = 3


def combined_all(value, axis, join):
    pieces = jax.tree.map(lambda part: lax.all_gather(part, axis), value)
    head = jax.tree.map(lambda part: part[0], pieces)
    tail = jax.tree.map(lambda part: part[1:], pieces)
    so_far, _ = lax.scan(lambda so_far, share: (join(so_far, share), None), head, tail)
    return so_far


def dense_blocks(columns, weights, width):
    positions = lax.broadcasted_iota(jnp.int32, (1, 1, width), 2)
    dense_block = jnp.zeros((columns.shape[0], columns.shape[2], width), jnp.bfloat16)
    for member in range(columns.shape[1]):
        dense_block = jnp.where(
            columns[:, member, :, None] == positions, weights[:, member, :, None], dense_block
        )
    return dense_block


def aligned_pieces(picked, columns, weights):
    slot_count = picked.shape[0]
    group_size = math.gcd(slot_count, 16)
    group_count = slot_count // group_size

    def one_group(inputs):
        chosen_in, columns_in, weights_in = inputs
        dense_block = dense_blocks(columns_in, weights_in, BLOCK)
        product = jnp.einsum(
            "gcr,gcd->grd", chosen_in, dense_block, preferred_element_type=jnp.float32
        )
        return product.astype(jnp.bfloat16)

    shaped = (
        picked.reshape((group_count, group_size) + picked.shape[1:]),
        columns.reshape((group_count, group_size) + columns.shape[1:]),
        weights.reshape((group_count, group_size) + weights.shape[1:]),
    )
    return lax.map(one_group, shaped).reshape(slot_count, picked.shape[2], BLOCK)


def collect(received, arrived, blocks_here):
    wanted = lax.broadcasted_iota(jnp.int32, (arrived.shape[0], blocks_here), 1)
    selector = (arrived[:, None] == wanted).astype(jnp.bfloat16)
    summed = jnp.einsum("srd,sj->rjd", received, selector, preferred_element_type=jnp.float32)
    return summed.reshape(received.shape[1], blocks_here * received.shape[2])


def local(hidden_rows, head_weight, block_links, teacher_rows, offsets, link_weights):
    halves = jnp.dot(
        lax.all_gather(hidden_rows, "vocab", axis=0, tiled=True),
        head_weight,
        preferred_element_type=jnp.float32,
    )
    logits = lax.psum_scatter(halves, "tok", scatter_dimension=0, tiled=True)
    local_peak = jnp.max(logits, axis=1)
    local_mass = jnp.sum(jnp.exp(logits - local_peak[:, None]), axis=1)

    def combine(earlier, later):
        top_value = jnp.maximum(earlier[0], later[0])
        joined = earlier[1] * jnp.exp(earlier[0] - top_value) + later[1] * jnp.exp(
            later[0] - top_value
        )
        return (top_value, joined)

    row_peak, row_mass = combined_all((local_peak, local_mass), "vocab", combine)
    exponent = jnp.exp(logits - row_peak[:, None])
    teacher_probs = (exponent / row_mass[:, None]).astype(jnp.bfloat16)
    by_column = teacher_probs.T
    columns_wanted = block_links[0][:, None] * BLOCK + teacher_rows
    picked = jnp.take(by_column, columns_wanted, axis=0)
    targets = block_links[1][:, None]
    pieces = aligned_pieces(picked, offsets, link_weights)
    received, arrived = (
        lax.all_to_all(pieces, "vocab", split_axis=0, concat_axis=0, tiled=True),
        lax.all_to_all(targets, "vocab", split_axis=0, concat_axis=0, tiled=True),
    )
    aligned = collect(received, arrived[:, 0], SB_DEV)
    row_total = lax.psum(jnp.sum(aligned, axis=1), "vocab")
    student_width = aligned.shape[1] * lax.axis_size("vocab")
    student_targets = student_width * aligned / row_total[:, None]
    return (row_peak + jnp.log(row_mass), student_targets)


def solution(mesh):
    placed = (
        P(("groups", "vocab"), "tok"),
        P("tok", "vocab"),
        P(None, "vocab"),
        P("vocab", None),
        P("vocab", None, None),
        P("vocab", None, None),
    )
    return jax.shard_map(
        local,
        mesh=mesh,
        in_specs=placed,
        out_specs=(P(("groups", "tok")), P(("groups", "tok"), "vocab")),
        check_vma=False,
    )
```

profile of v0, /device:TPU:0, one launch (start us, length us, event | category | flops | bytes accessed | tf_op | source)
XLA Modules:
  0.0 160.6 jit_solution(5689754027078589438)
XLA Ops:
  7.2 0.0 copy-start
  7.2 0.0 all-gather.6.cloned.1.call-start
  7.2 0.7 all-gather.6.cloned.1.call-update
  7.9 0.0 copy-start.4
  7.9 0.0 copy-start.3
  7.9 0.0 copy-start.1
  7.9 0.0 copy-start.2
  8.0 0.0 reduce-scatter.2.cloned.1.call-start
  8.0 45.0 %all-gather.6.cloned.1.call-done = bf16[256,2048]{1,0:T(8,128)(2,1)} async-done(((bf16[32,2048]{1,0:T(8,128)(2,1)}), bf16[256,2048]{1,0:T(8,128)(2,1)}) %all-gather.6.cloned.1.call-update) | async-done | bytes 1048592 | tf_op jit(solution)/shard_map/all_gather | solution.py:60
  53.0 0.0 copy-done
  53.0 3.1 %fusion.38 = f32[256,768]{1,0:T(8,128)} fusion(bf16[256,2048]{1,0:T(8,128)(2,1)} %all-gather.6.cloned.1.call-done, bf16[2048,768]{1,0:T(8,128)(2,1)S(1)} %copy-done), kind=kOutput, calls=%fused_computation.58 | convolution fusion | flops 805306368 | bytes 4980736 | tf_op jit(solution)/shard_map/dot_general | solution.py:59
  56.1 0.0 reduce-scatter.2.cloned.1.call-update
  56.2 0.0 copy-done.4
  56.2 0.7 copy.26
  56.9 3.4 %all-to-all-start = ((s32[8,1,1]{2,1,0:T(1,128)}), s32[8,1,1]{2,1,0:T(1,128)S(1)}, u32[]{:S(2)}, u32[]{:S(2)}) async-start(s32[8,1,1]{2,1,0:T(1,128)} %copy.26), calls=%async_computation.1 | async-start | bytes 8192 | tf_op jit(solution)/shard_map/all_to_all | solution.py:85
  60.2 0.0 copy-done.3
  60.2 0.7 compare_and_fusion
  60.9 0.0 copy-done.1
  60.9 0.6 copy_bitcast_fusion.2
  61.5 0.6 copy_bitcast_fusion.4
  62.1 0.1 bitcast_clamp_fusion
  62.1 0.0 copy-done.2
  62.1 0.6 fusion.32
  62.8 0.6 reduce-scatter.2.cloned.1.call-done
  63.3 1.1 reduce_max.9
  64.4 1.2 exponential_reduce_fusion
  65.6 20.6 %all-gather.3 = f32[8,1,128]{2,1,0:T(1,128)S(1)} all-gather(f32[1,1,128]{2,1,0:T(1,128)S(1)} %bitcast.67), channel_id=3, replica_groups=mesh['groups'=2,'vocab'=8,'tok'=2] {'vocab'}, dimensions={0}, use_global_device_ids=true | all-gather | bytes 4608 | tf_op jit(solution)/shard_map/all_gather | solution.py:13
  86.3 16.1 %all-gather.2 = f32[8,1,128]{2,1,0:T(1,128)S(1)} all-gather(f32[1,1,128]{2,1,0:T(1,128)S(1)} %bitcast.62), channel_id=2, replica_groups=mesh['groups'=2,'vocab'=8,'tok'=2] {'vocab'}, dimensions={0}, use_global_device_ids=true | all-gather | bytes 4608 | tf_op jit(solution)/shard_map/all_gather | solution.py:13
  102.4 0.3 while.3
  102.7 1.1 fusion.23
  103.9 0.2 copy.27
  104.1 4.3 %gather_fusion = bf16[1024,128]{1,0:T(8,128)(2,1)} fusion(bf16[768,128]{1,0:T(8,128)(2,1)S(1)} %copy.27, s32[1024]{0:T(1024)S(1)} %bitcast_clamp_fusion), kind=kCustom, calls=%fused_computation | custom fusion | bytes 528384 | tf_op jit(solution)/shard_map/jit(_take)/gather | solution.py:80
  108.4 1.1 copy.28
  109.5 3.6 %convolution_convert_fusion = bf16[8,128,256]{2,1,0:T(8,128)(2,1)} fusion(s32[8,128]{1,0:T(8,128)} %bitcast.65, s32[8,128]{1,0:T(8,128)} %bitcast.66, s32[8,128]{1,0:T(8,128)} %bitcast.64, s32[8,128]{1,0:T(8,128)} %bitcast.63, bf16[8,128]{1,0:T(8,128)(2,1)} %get-tuple-element.77, bf16[8,128]{1,0:T(8,128)(2,1)} %get-tuple-element.78, ...), kind=kOutput, calls=%fused_computation.8 | convolution fusion | flops 69599232 | bytes 812032 | tf_op jit(solution)/shard_map/while/body/eval_jaxpr/gcr,gcd->grd/dot_general | solution.py:38
  113.1 0.0 all-to-all-done
  113.1 4.2 %all-to-all-start.1 = ((bf16[8,128,256]{2,1,0:T(8,128)(2,1)}), bf16[8,128,256]{2,1,0:T(8,128)(2,1)}, u32[]{:S(2)}, u32[]{:S(2)}) async-start(bf16[8,128,256]{2,1,0:T(8,128)(2,1)} %convolution_convert_fusion), calls=%async_computation.2 | async-start | bytes 1048576 | tf_op jit(solution)/shard_map/all_to_all | solution.py:84
  117.3 0.2 reduce.2
  117.5 0.5 log_add_fusion
  118.1 9.5 %all-to-all-done.1 = bf16[8,128,256]{2,1,0:T(8,128)(2,1)} async-done(((bf16[8,128,256]{2,1,0:T(8,128)(2,1)}), bf16[8,128,256]{2,1,0:T(8,128)(2,1)}, u32[]{:S(2)}, u32[]{:S(2)}) %all-to-all-start.1) | async-done | bytes 524320 | tf_op jit(solution)/shard_map/all_to_all | solution.py:84
  127.6 2.8 %fusion.31 = (f32[128]{0:T(128)S(1)}, f32[128,3,256]{2,1,0:T(4,128)}) fusion(bf16[8,128,256]{2,1,0:T(8,128)(2,1)} %all-to-all-done.1, s32[8]{0:T(128)S(1)} %reduce.2), kind=kOutput, calls=%fused_computation.55 | convolution fusion | flops 1769368 | bytes 918048 | tf_op jit(solution)/shard_map/srd,sj->rjd/dot_general | solution.py:54
  130.3 1.2 copy.34
  131.5 19.6 %psum.7 = f32[128]{0:T(128)S(1)} all-reduce(f32[128]{0:T(128)S(1)} %get-tuple-element.65), channel_id=1, replica_groups=mesh['groups'=2,'vocab'=8,'tok'=2] {'vocab'}, use_global_device_ids=true, to_apply=%region_6.7 | all-reduce | flops 128 | bytes 1024 | tf_op jit(solution)/shard_map/psum | solution.py:88
  151.1 0.8 bitcast_divide_fusion
  151.9 1.9 %copy.35 = f32[128,768]{1,0:T(8,128)} copy(f32[128,768]{0,1:T(8,128)} %bitcast_divide_fusion) | data formatting | bytes 786432
  (15 shorter events, 0.2 us)
Async XLA Ops:
  7.2 45.9 %copy-start = (bf16[2048,768]{1,0:T(8,128)(2,1)S(1)}, bf16[2048,768]{1,0:T(8,128)(2,1)}, u32[]{:S(2)}) copy-start(bf16[2048,768]{1,0:T(8,128)(2,1)} %param.9) | copy-start | bytes 9437188
  7.2 45.8 %all-gather.6.cloned.1.call-start = ((), (), s32[]{:S(2)}) async-start(), calls=%async_computation.3 | async-start | bytes 1179648 | tf_op jit(solution)/shard_map/all_gather | solution.py:60
  7.9 48.3 %copy-start.4 = (s32[2,8]{1,0:T(2,128)S(1)}, s32[2,8]{1,0:T(2,128)}, u32[]{:S(2)}) copy-start(s32[2,8]{1,0:T(2,128)} %param.10) | copy-start | bytes 196
  7.9 52.3 %copy-start.3 = (s32[8,128]{1,0:T(8,128)S(1)}, s32[8,128]{1,0:T(8,128)}, u32[]{:S(2)}) copy-start(s32[8,128]{1,0:T(8,128)} %param.11) | copy-start | bytes 12292
  7.9 52.9 %copy-start.1 = (bf16[8,4,128]{2,1,0:T(4,128)(2,1)S(1)}, bf16[8,4,128]{2,1,0:T(4,128)(2,1)}, u32[]{:S(2)}) copy-start(bf16[8,4,128]{2,1,0:T(4,128)(2,1)} %param.13) | copy-start | bytes 24580
  7.9 54.2 %copy-start.2 = (s32[8,4,128]{2,1,0:T(4,128)S(1)}, s32[8,4,128]{2,1,0:T(4,128)}, u32[]{:S(2)}) copy-start(s32[8,4,128]{2,1,0:T(4,128)} %param.12) | copy-start | bytes 49156
  8.0 55.4 %reduce-scatter.2.cloned.1.call-start = ((), (), s32[]{:S(2)}) async-start(), calls=%async_computation.4 | async-start | bytes 1179648 | tf_op jit(solution)/shard_map/reduce_scatter | solution.py:64
  56.9 56.3 %all-to-all-start = ((s32[8,1,1]{2,1,0:T(1,128)}), s32[8,1,1]{2,1,0:T(1,128)S(1)}, u32[]{:S(2)}, u32[]{:S(2)}) async-start(s32[8,1,1]{2,1,0:T(1,128)} %copy.26), calls=%async_computation.1 | async-start | bytes 8192 | tf_op jit(solution)/shard_map/all_to_all | solution.py:85
  113.1 14.4 %all-to-all-start.1 = ((bf16[8,128,256]{2,1,0:T(8,128)(2,1)}), bf16[8,128,256]{2,1,0:T(8,128)(2,1)}, u32[]{:S(2)}, u32[]{:S(2)}) async-start(bf16[8,128,256]{2,1,0:T(8,128)(2,1)} %convolution_convert_fusion), calls=%async_computation.2 | async-start | bytes 1048576 | tf_op jit(solution)/shard_map/all_to_all | solution.py:84
Sparse Core Ops, SparseCore 0:
  10.1 42.8 all-gather.5
  56.3 6.9 reduce-scatter.1
where the time goes:
time: 161 us
  blocking collectives  56.3 us (35%)
  waiting for transfers between devices  55.8 us (35%)
  between operations  14.2 us (9%)
  local copies, waits for them, and re-layouts  11.2 us (7%)
  matrix products  9.5 us (6%)
  starting transfers between devices  7.58 us (5%)
  other arithmetic  5.94 us (4%)
    all_gather x1, waiting for transfers between devices, local(): lax.all_gather(hidden_rows, 'vocab', axis=0, tiled=True)  45 us
    all_gather x2, blocking collectives, combined_all(): pieces = jax.tree.map(lambda part: lax.all_gather(part, axis), value)  36.8 us
    psum x1, blocking collectives, local(): row_total = lax.psum(jnp.sum(aligned, axis=1), 'vocab')  19.6 us
    all_to_all x1, waiting for transfers between devices, local(): lax.all_to_all(pieces, 'vocab', split_axis=0, concat_axis=0, tiled=True)  9.51 us
    gather x2, local copies, waits for them, and re-layouts, local(): picked = jnp.take(by_column, columns_wanted, axis=0)  5.43 us
    all_to_all x1, starting transfers between devices, local(): lax.all_to_all(pieces, 'vocab', split_axis=0, concat_axis=0, tiled=True)  4.15 us
    dot_general x1, matrix products, one_group(): jnp.einsum('gcr,gcd->grd', chosen_in, dense_block, preferred_element_type...  3.63 us
    all_to_all x1, starting transfers between devices, local(): lax.all_to_all(targets, 'vocab', split_axis=0, concat_axis=0, tiled=True)  3.36 us
  transfers between devices with their start and end apart: 4, of which 3 were waited for; matrix products, arithmetic and copies ran while one was open for 10% of the time, Pallas kernels for 0%

commit v1 on v0

--- a/solution.py
+++ b/solution.py
@@ -1,8 +1,11 @@
+import functools
 import math
 
 import jax
 import jax.numpy as jnp
 from jax import lax
+from jax.experimental import pallas as pl
+from jax.experimental.pallas import tpu as pltpu
 from jax.sharding import PartitionSpec as P
 
 BLOCK = 256
@@ -91,6 +94,346 @@
     return (row_peak + jnp.log(row_mass), student_targets)
 
 
+MESH = pl.DeviceIdType.MESH
+
+
+def fused_kernel(
+    n,
+    hidden_ref,
+    weight_ref,
+    links_ref,
+    rows_ref,
+    offsets_ref,
+    link_weights_ref,
+    log_ref,
+    target_ref,
+    held,
+    weight,
+    own_half,
+    other_half,
+    arrived_half,
+    exponents,
+    onehot,
+    meta_out,
+    meta_in,
+    dense,
+    used_out,
+    used_in,
+    stats_out,
+    stats_in,
+    local_sems,
+    hidden_send,
+    hidden_recv,
+    meta_send,
+    meta_recv,
+    half_send,
+    half_recv,
+    used_send,
+    used_recv,
+    stats_send,
+    stats_recv,
+):
+    group, me, tok = lax.axis_index("groups"), lax.axis_index("vocab"), lax.axis_index("tok")
+    columns = weight.shape[1]
+    tiles = columns // BLOCK
+    half_blocks = n // 2
+    tokens = own_half.shape[0]
+    used = rows_ref.shape[1]
+
+    def peer(index):
+        return (group, index, tok)
+
+    sibling = (group, me, 1 - tok)
+
+    def remote(source, target, send, recv, device):
+        return pltpu.make_async_remote_copy(
+            src_ref=source,
+            dst_ref=target,
+            send_sem=send,
+            recv_sem=recv,
+            device_id=device,
+            device_id_type=MESH,
+        )
+
+    def others():
+        return [lax.rem(me + step, n) for step in range(1, n)]
+
+    barrier = pltpu.get_barrier_semaphore()
+    for other in others():
+        pl.semaphore_signal(barrier, inc=1, device_id=peer(other), device_id_type=MESH)
+    pl.semaphore_signal(barrier, inc=1, device_id=sibling, device_id_type=MESH)
+    weight_copy = pltpu.make_async_copy(weight_ref, weight, local_sems.at[0])
+    weight_copy.start()
+    own_copy = pltpu.make_async_copy(hidden_ref, held.at[me], local_sems.at[1])
+    own_copy.start()
+    values = link_weights_ref[...].astype(jnp.float32)
+    for slot in range(n):
+        place = offsets_ref[slot] + links_ref[1, slot] * BLOCK
+        meta_out[slot, 0:4, :] = place.astype(jnp.float32)
+        meta_out[slot, 4:8, :] = values[slot]
+    pl.semaphore_wait(barrier, n)
+
+    across = me + 1 - 2 * lax.rem(me, 2)
+    line = [lax.rem(me + 2 * step, n) for step in range(1, n // 2)]
+    sends = []
+
+    def launch(copy):
+        copy.start()
+        sends.append(copy)
+
+    launch(remote(hidden_ref, held.at[me], hidden_send.at[0], hidden_recv.at[me], peer(across)))
+    for step, other in enumerate(line):
+        launch(
+            remote(
+                hidden_ref,
+                held.at[me],
+                hidden_send.at[1 + step],
+                hidden_recv.at[me],
+                peer(other),
+            )
+        )
+    for step, other in enumerate(others()):
+        launch(
+            remote(
+                meta_out.at[other],
+                meta_in.at[me],
+                meta_send.at[step],
+                meta_recv.at[me],
+                peer(other),
+            )
+        )
+    meta_in[me] = meta_out[me]
+
+    row_index = lax.broadcasted_iota(jnp.int32, (BLOCK, used), 0)
+    for slot in range(n):
+        onehot[slot] = (rows_ref[slot : slot + 1, :] == row_index).astype(jnp.bfloat16)
+
+    def wait_hidden(source):
+        remote(
+            held.at[source], held.at[source], hidden_send.at[0], hidden_recv.at[source], sibling
+        ).wait_recv()
+
+    for step, other in enumerate(line):
+        wait_hidden(other)
+        launch(
+            remote(
+                held.at[other],
+                held.at[other],
+                hidden_send.at[n // 2 + step],
+                hidden_recv.at[other],
+                peer(across),
+            )
+        )
+
+    place_index = lax.broadcasted_iota(jnp.int32, (BLOCK, used), 0).astype(jnp.float32)
+
+    def build_dense(source):
+        meta = meta_in[source]
+        for tile in range(tiles):
+            block = jnp.zeros((BLOCK, used), jnp.float32)
+            for member in range(4):
+                place = meta[member : member + 1, :] - float(tile * BLOCK)
+                block = jnp.where(place == place_index, meta[4 + member : 5 + member, :], block)
+            dense[source, tile * BLOCK : (tile + 1) * BLOCK, :] = block.astype(jnp.bfloat16)
+
+    for other in others():
+        remote(
+            meta_in.at[other], meta_in.at[other], meta_send.at[0], meta_recv.at[other], sibling
+        ).wait_recv()
+        build_dense(other)
+    build_dense(me)
+
+    weight_copy.wait()
+    own_copy.wait()
+    wait_hidden(across)
+    for other in line:
+        wait_hidden(other + across - me)
+
+    def half_rows(which):
+        blocks = held[pl.ds(which * half_blocks, half_blocks)]
+        return blocks.reshape(tokens, blocks.shape[2])
+
+    for tile in range(tiles):
+        cut = slice(tile * BLOCK, (tile + 1) * BLOCK)
+        other_half[tile] = jnp.dot(
+            half_rows(1 - tok), weight[:, cut], preferred_element_type=jnp.float32
+        )
+        launch(
+            remote(
+                other_half.at[tile],
+                arrived_half.at[tile],
+                half_send.at[tile],
+                half_recv.at[tile],
+                sibling,
+            )
+        )
+    for tile in range(tiles):
+        cut = slice(tile * BLOCK, (tile + 1) * BLOCK)
+        own_half[:, cut] = jnp.dot(
+            half_rows(tok), weight[:, cut], preferred_element_type=jnp.float32
+        )
+    for tile in range(tiles):
+        cut = slice(tile * BLOCK, (tile + 1) * BLOCK)
+        remote(
+            other_half.at[tile],
+            arrived_half.at[tile],
+            half_send.at[tile],
+            half_recv.at[tile],
+            sibling,
+        ).wait_recv()
+        own_half[:, cut] = own_half[:, cut] + arrived_half[tile]
+
+    logits = own_half[...]
+    peak = jnp.max(logits, axis=1, keepdims=True)
+    exponent = jnp.exp(logits - peak)
+    mass = jnp.sum(exponent, axis=1, keepdims=True)
+    for tile in range(tiles):
+        exponents[tile] = exponent[:, tile * BLOCK : (tile + 1) * BLOCK].astype(jnp.bfloat16)
+
+    running = jnp.zeros((tokens, used), jnp.float32)
+    for step, other in enumerate(others() + [me]):
+        picked = jnp.dot(
+            exponents[links_ref[0, other]], onehot[other], preferred_element_type=jnp.float32
+        )
+        meta = meta_out[other]
+        gain = jnp.sum(
+            jnp.where(meta[0:4] >= 0.0, meta[4:8], 0.0), axis=0, keepdims=True
+        )
+        running = running + picked * gain
+        if step < n - 1:
+            used_out[step] = picked.astype(jnp.bfloat16)
+            launch(
+                remote(
+                    used_out.at[step],
+                    used_in.at[me],
+                    used_send.at[step],
+                    used_recv.at[me],
+                    peer(other),
+                )
+            )
+        else:
+            used_in[me] = picked.astype(jnp.bfloat16)
+    total = jnp.sum(running, axis=1, keepdims=True)
+
+    lane = lax.broadcasted_iota(jnp.int32, (tokens, 128), 1)
+    packed = jnp.where(lane == 0, peak, jnp.where(lane == 1, mass, total))
+    stats_out[...] = packed.T[0:8, :]
+    for step, other in enumerate(others()):
+        launch(
+            remote(
+                stats_out,
+                stats_in.at[me],
+                stats_send.at[step],
+                stats_recv.at[me],
+                peer(other),
+            )
+        )
+    stats_in[me] = stats_out[...]
+
+    for other in others():
+        remote(
+            stats_out, stats_in.at[other], stats_send.at[0], stats_recv.at[other], sibling
+        ).wait_recv()
+
+    peaks = jnp.concatenate([stats_in[v, 0:1, :] for v in range(n)], axis=0)
+    masses = jnp.concatenate([stats_in[v, 1:2, :] for v in range(n)], axis=0)
+    totals = jnp.concatenate([stats_in[v, 2:3, :] for v in range(n)], axis=0)
+    row_peak = jnp.max(peaks, axis=0, keepdims=True)
+    shrink = jnp.exp(peaks - row_peak)
+    row_mass = jnp.sum(shrink * masses, axis=0, keepdims=True)
+    log_ref[...] = row_peak + jnp.log(row_mass)
+    share = shrink / row_mass
+    row_total = jnp.sum(share * totals, axis=0, keepdims=True)
+    factor = float(columns * n) * share / row_total
+    factors = jnp.concatenate([factor, jnp.zeros((128 - n, tokens), jnp.float32)], axis=0).T
+
+    for other in others():
+        remote(
+            used_in.at[other], used_in.at[other], used_send.at[0], used_recv.at[other], sibling
+        ).wait_recv()
+    for tile in range(tiles):
+        cut = slice(tile * BLOCK, (tile + 1) * BLOCK)
+        block = jnp.zeros((tokens, BLOCK), jnp.float32)
+        for v in range(n):
+            piece = lax.dot_general(
+                used_in[v],
+                dense[v, cut, :],
+                (((1,), (1,)), ((), ())),
+                preferred_element_type=jnp.float32,
+            )
+            block = block + factors[:, v : v + 1] * piece
+        target_ref[:, cut] = block
+
+    for copy in sends:
+        copy.wait_send()
+
+
+def fused(hidden_rows, head_weight, block_links, teacher_rows, offsets, link_weights):
+    n = lax.axis_size("vocab")
+    rows, depth = hidden_rows.shape
+    columns = head_weight.shape[1]
+    tiles = columns // BLOCK
+    tokens = rows * n // 2
+    used = teacher_rows.shape[1]
+    dma = pltpu.SemaphoreType.DMA
+    vmem = pl.BlockSpec(memory_space=pltpu.VMEM)
+    log_partition, student_targets = pl.pallas_call(
+        functools.partial(fused_kernel, n),
+        out_shape=(
+            jax.ShapeDtypeStruct((1, tokens), jnp.float32),
+            jax.ShapeDtypeStruct((tokens, columns), jnp.float32),
+        ),
+        in_specs=[
+            pl.BlockSpec(memory_space=pl.ANY),
+            pl.BlockSpec(memory_space=pl.ANY),
+            pl.BlockSpec(memory_space=pltpu.SMEM),
+            vmem,
+            vmem,
+            vmem,
+        ],
+        out_specs=(vmem, vmem),
+        scratch_shapes=[
+            pltpu.VMEM((n, rows, depth), jnp.bfloat16),
+            pltpu.VMEM((depth, columns), jnp.bfloat16),
+            pltpu.VMEM((tokens, columns), jnp.float32),
+            pltpu.VMEM((tiles, tokens, BLOCK), jnp.float32),
+            pltpu.VMEM((tiles, tokens, BLOCK), jnp.float32),
+            pltpu.VMEM((tiles, tokens, BLOCK), jnp.bfloat16),
+            pltpu.VMEM((n, BLOCK, used), jnp.bfloat16),
+            pltpu.VMEM((n, 8, used), jnp.float32),
+            pltpu.VMEM((n, 8, used), jnp.float32),
+            pltpu.VMEM((n, columns, used), jnp.bfloat16),
+            pltpu.VMEM((n - 1, tokens, used), jnp.bfloat16),
+            pltpu.VMEM((n, tokens, used), jnp.bfloat16),
+            pltpu.VMEM((8, tokens), jnp.float32),
+            pltpu.VMEM((n, 8, tokens), jnp.float32),
+            dma((2,)),
+            dma((n - 1,)),
+            dma((n,)),
+            dma((n - 1,)),
+            dma((n,)),
+            dma((tiles,)),
+            dma((tiles,)),
+            dma((n - 1,)),
+            dma((n,)),
+            dma((n - 1,)),
+            dma((n,)),
+        ],
+        compiler_params=pltpu.CompilerParams(
+            collective_id=0, has_side_effects=True, vmem_limit_bytes=32 * 1024 * 1024
+        ),
+    )(hidden_rows, head_weight, block_links, teacher_rows, offsets, link_weights)
+    return log_partition.reshape(tokens), student_targets
+
+
+def head(hidden_rows, head_weight, block_links, teacher_rows, offsets, link_weights):
+    n = lax.axis_size("vocab")
+    rows = hidden_rows.shape[0]
+    fits = rows % 16 == 0 and rows * n == 256 and n % 2 == 0 and teacher_rows.shape[0] == n
+    form = fused if fits and lax.axis_size("tok") == 2 and n <= 16 else local
+    return form(hidden_rows, head_weight, block_links, teacher_rows, offsets, link_weights)
+
+
 def solution(mesh):
     placed = (
         P(("groups", "vocab"), "tok"),
@@ -101,7 +444,7 @@
         P("vocab", None, None),
     )
     return jax.shard_map(
-        local,
+        head,
         mesh=mesh,
         in_specs=placed,
         out_specs=(P(("groups", "tok")), P(("groups", "tok"), "vocab")),

time: 161 us -> 47 us (0.29)
  blocking collectives: 56.3 us -> 0 us
  waiting for transfers between devices: 55.8 us -> 0 us
  Pallas kernels: 0 us -> 39.2 us
  between operations: 14.2 us -> 0.65 us
  matrix products: 9.5 us -> 0 us
  starting transfers between devices: 7.58 us -> 0 us
  other arithmetic: 5.94 us -> 0 us
  local copies, waits for them, and re-layouts: 11.2 us -> 6.82 us
    all_gather x1 -> x0, waiting for transfers between devices: 45 us -> none  [local(): lax.all_gather(hidden_rows, 'vocab', axis=0, tiled=True)]
    pallas_call x0 -> x1, Pallas kernels: none -> 39.2 us  [fused(): pl.pallas_call(functools.partial(fused_kernel, n), out_shape=(jax.ShapeDt...]
    all_gather x2 -> x0, blocking collectives: 36.8 us -> none  [combined_all(): pieces = jax.tree.map(lambda part: lax.all_gather(part, axis), value)]
    psum x1 -> x0, blocking collectives: 19.6 us -> none  [local(): row_total = lax.psum(jnp.sum(aligned, axis=1), 'vocab')]
    all_to_all x2 -> x0, waiting for transfers between devices: 9.52 us -> none  [the longest x1 9.51 us: local(): lax.all_to_all(pieces, 'vocab', split_axis=0, concat_axis=0, tiled=True)]
    dot_general x3 -> x0, matrix products: 9.5 us -> none  [the longest x1 3.63 us: one_group(): jnp.einsum('gcr,gcd->grd', chosen_in, dense_block, preferred_element_type...]
    all_to_all x2 -> x0, starting transfers between devices: 7.51 us -> none  [the longest x1 4.15 us: local(): lax.all_to_all(pieces, 'vocab', split_axis=0, concat_axis=0, tiled=True)]
    gather x2 -> x0, local copies, waits for them, and re-layouts: 5.43 us -> none  [local(): picked = jnp.take(by_column, columns_wanted, axis=0)]
  transfers between devices with their start and end apart: 4 -> 0, of which waited for: 3 -> 0; matrix products, arithmetic and copies ran while one was open for 10% -> 0% of each run, Pallas kernels for 0% -> 0%
where the time goes in v1:
time: 47 us; the launch traced here: 46.6 us
  Pallas kernels  39.2 us (83%)
  local copies, waits for them, and re-layouts  6.82 us (15%)
  between operations  0.65 us (1%)
    pallas_call x1, Pallas kernels, fused(): pl.pallas_call(functools.partial(fused_kernel, n), out_shape=(jax.ShapeDt...  39.2 us
    unnamed x14, local copies, waits for them, and re-layouts  6.82 us

profile of v1, /device:TPU:0, one launch (start us, length us, event | category | flops | bytes accessed | tf_op | source)
XLA Modules:
  0.0 46.6 jit_solution(11191137314509570416)
XLA Ops:
  0.6 0.0 copy-start
  0.6 1.9 %copy-done = bf16[2048,768]{1,0:T(8,128)(2,1)S(1)} copy-done((bf16[2048,768]{1,0:T(8,128)(2,1)S(1)}, bf16[2048,768]{1,0:T(8,128)(2,1)}, u32[]{:S(2)}) %copy-start) | copy-done | bytes 3145752
  2.5 0.0 copy-start.1
  2.5 0.9 %copy-done.1 = bf16[32,2048]{1,0:T(8,128)(2,1)S(1)} copy-done((bf16[32,2048]{1,0:T(8,128)(2,1)S(1)}, bf16[32,2048]{1,0:T(8,128)(2,1)}, u32[]{:S(2)}) %copy-start.1) | copy-done | bytes 131096
  3.4 0.0 copy-start.2
  3.4 0.7 %copy-done.2 = s32[8,4,128]{2,1,0:T(4,128)S(1)} copy-done((s32[8,4,128]{2,1,0:T(4,128)S(1)}, s32[8,4,128]{2,1,0:T(4,128)}, u32[]{:S(2)}) %copy-start.2) | copy-done | bytes 16408
  4.1 0.0 copy-start.3
  4.1 0.7 %copy-done.3 = bf16[8,4,128]{2,1,0:T(4,128)(2,1)S(1)} copy-done((bf16[8,4,128]{2,1,0:T(4,128)(2,1)S(1)}, bf16[8,4,128]{2,1,0:T(4,128)(2,1)}, u32[]{:S(2)}) %copy-start.3) | copy-done | bytes 8216
  4.8 0.0 copy-start.4
  4.8 0.7 %copy-done.4 = s32[8,128]{1,0:T(8,128)S(1)} copy-done((s32[8,128]{1,0:T(8,128)S(1)}, s32[8,128]{1,0:T(8,128)}, u32[]{:S(2)}) %copy-start.4) | copy-done | bytes 4120
  5.5 0.0 copy-start.5
  5.5 0.7 %copy-done.5 = s32[2,8]{1,0:T(2,128)S(1)} copy-done((s32[2,8]{1,0:T(2,128)S(1)}, s32[2,8]{1,0:T(2,128)}, u32[]{:S(2)}) %copy-start.5) | copy-done | bytes 88
  6.2 39.2 %shard_map.77 = (f32[1,128]{1,0:T(1,128)S(1)}, f32[128,768]{1,0:T(8,128)S(1)}) custom-call(bf16[32,2048]{1,0:T(8,128)(2,1)S(1)} %copy-done.1, bf16[2048,768]{1,0:T(8,128)(2,1)S(1)} %copy-done, s32[2,8]{1,0:T(2,128)S(1)} %copy-done.5, s32[8,128]{1,0:T(8,128)S(1)} %copy-done.4, s32[8,4,128]{2,1,0:T(4,128)S(1)} %copy-done.2, bf16[8,4,128]{2,1,0:T(4,128)(2,1)S(1)} %copy-done.3), custom_call_target="tpu_custom_call" | custom-call | tf_op jit(solution)/shard_map/pallas_call | solution.py:380
  45.4 0.5 %copy.10 = f32[128]{0:T(128)} copy(f32[128]{0:T(128)S(1)} %bitcast.1) | data formatting | bytes 1024
  45.9 0.7 %copy.11 = f32[128,768]{1,0:T(8,128)} copy(f32[128,768]{1,0:T(8,128)S(1)} %get-tuple-element.9) | data formatting | bytes 786432
Async XLA Ops:
  0.6 1.9 %copy-start = (bf16[2048,768]{1,0:T(8,128)(2,1)S(1)}, bf16[2048,768]{1,0:T(8,128)(2,1)}, u32[]{:S(2)}) copy-start(bf16[2048,768]{1,0:T(8,128)(2,1)} %weight_ref.1) | copy-start | bytes 9437188
  2.5 0.9 %copy-start.1 = (bf16[32,2048]{1,0:T(8,128)(2,1)S(1)}, bf16[32,2048]{1,0:T(8,128)(2,1)}, u32[]{:S(2)}) copy-start(bf16[32,2048]{1,0:T(8,128)(2,1)} %hidden_ref.1) | copy-start | bytes 393220
  3.4 0.7 %copy-start.2 = (s32[8,4,128]{2,1,0:T(4,128)S(1)}, s32[8,4,128]{2,1,0:T(4,128)}, u32[]{:S(2)}) copy-start(s32[8,4,128]{2,1,0:T(4,128)} %offsets_ref.1) | copy-start | bytes 49156
  4.1 0.7 %copy-start.3 = (bf16[8,4,128]{2,1,0:T(4,128)(2,1)S(1)}, bf16[8,4,128]{2,1,0:T(4,128)(2,1)}, u32[]{:S(2)}) copy-start(bf16[8,4,128]{2,1,0:T(4,128)(2,1)} %link_weights_ref.1) | copy-start | bytes 24580
  4.8 0.7 %copy-start.4 = (s32[8,128]{1,0:T(8,128)S(1)}, s32[8,128]{1,0:T(8,128)}, u32[]{:S(2)}) copy-start(s32[8,128]{1,0:T(8,128)} %rows_ref.1) | copy-start | bytes 12292
  5.5 0.7 %copy-start.5 = (s32[2,8]{1,0:T(2,128)S(1)}, s32[2,8]{1,0:T(2,128)}, u32[]{:S(2)}) copy-start(s32[2,8]{1,0:T(2,128)} %links_ref.1) | copy-start | bytes 196

commit v2 on v1

--- a/solution.py
+++ b/solution.py
@@ -9,6 +9,7 @@
 from jax.sharding import PartitionSpec as P
 
 BLOCK = 256
+CHUNKS = 2
 SB_DEV = 3
 
 
@@ -101,12 +102,16 @@
     n,
     hidden_ref,
     weight_ref,
+    links_hbm,
+    rows_hbm,
+    offsets_hbm,
+    link_weights_hbm,
+    log_ref,
+    target_ref,
     links_ref,
     rows_ref,
     offsets_ref,
     link_weights_ref,
-    log_ref,
-    target_ref,
     held,
     weight,
     own_half,
@@ -158,40 +163,105 @@
     def others():
         return [lax.rem(me + step, n) for step in range(1, n)]
 
+    across = me + 1 - 2 * lax.rem(me, 2)
+    place_z, last_z = me // 2, n // 2 - 1
+    has_lower, has_upper = place_z > 0, place_z < last_z
+
     barrier = pltpu.get_barrier_semaphore()
-    for other in others():
-        pl.semaphore_signal(barrier, inc=1, device_id=peer(other), device_id_type=MESH)
-    pl.semaphore_signal(barrier, inc=1, device_id=sibling, device_id_type=MESH)
+    for other in (peer(across), sibling):
+        pl.semaphore_signal(barrier, inc=1, device_id=other, device_id_type=MESH)
+
+    @pl.when(has_lower)
+    def greet_lower():
+        pl.semaphore_signal(barrier, inc=1, device_id=peer(me - 2), device_id_type=MESH)
+
+    @pl.when(has_upper)
+    def greet_upper():
+        pl.semaphore_signal(barrier, inc=1, device_id=peer(me + 2), device_id_type=MESH)
+
     weight_copy = pltpu.make_async_copy(weight_ref, weight, local_sems.at[0])
     weight_copy.start()
     own_copy = pltpu.make_async_copy(hidden_ref, held.at[me], local_sems.at[1])
     own_copy.start()
+    small_copies = [
+        pltpu.make_async_copy(source, target, local_sems.at[2 + index])
+        for index, (source, target) in enumerate(
+            (
+                (links_hbm, links_ref),
+                (rows_hbm, rows_ref),
+                (offsets_hbm, offsets_ref),
+                (link_weights_hbm, link_weights_ref),
+            )
+        )
+    ]
+    for copy in small_copies:
+        copy.start()
+    pl.semaphore_wait(barrier, 2 + (has_lower).astype(jnp.int32) + (has_upper).astype(jnp.int32))
+
+    sends = []
+
+    def launch(copy, live=None):
+        sends.append((copy, live))
+        if live is None:
+            copy.start()
+        else:
+            pl.when(live)(copy.start)
+
+    part = held.shape[1] // CHUNKS
+
+    def held_part(source, chunk):
+        return held.at[source, pl.ds(chunk * part, part)]
+
+    def hidden_copy(source, chunk, send, target, own=False):
+        here = hidden_ref.at[pl.ds(chunk * part, part)] if own else held_part(source, chunk)
+        return remote(
+            here,
+            held_part(source, chunk),
+            hidden_send.at[send * CHUNKS + chunk],
+            hidden_recv.at[source * CHUNKS + chunk],
+            peer(target),
+        )
+
+    for chunk in range(CHUNKS):
+        launch(hidden_copy(me, chunk, 1, me - 2, True), has_lower)
+        launch(hidden_copy(me, chunk, 2, me + 2, True), has_upper)
+        launch(hidden_copy(me, chunk, 0, across, True))
+
+    for copy in small_copies:
+        copy.wait()
     values = link_weights_ref[...].astype(jnp.float32)
     for slot in range(n):
         place = offsets_ref[slot] + links_ref[1, slot] * BLOCK
         meta_out[slot, 0:4, :] = place.astype(jnp.float32)
         meta_out[slot, 4:8, :] = values[slot]
-    pl.semaphore_wait(barrier, n)
-
-    across = me + 1 - 2 * lax.rem(me, 2)
-    line = [lax.rem(me + 2 * step, n) for step in range(1, n // 2)]
-    sends = []
-
-    def launch(copy):
-        copy.start()
-        sends.append(copy)
-
-    launch(remote(hidden_ref, held.at[me], hidden_send.at[0], hidden_recv.at[me], peer(across)))
-    for step, other in enumerate(line):
-        launch(
-            remote(
-                hidden_ref,
-                held.at[me],
-                hidden_send.at[1 + step],
-                hidden_recv.at[me],
-                peer(other),
-            )
-        )
+    meta_in[me] = meta_out[me]
+
+    row_index = lax.broadcasted_iota(jnp.int32, (BLOCK, used), 0)
+    for slot in range(n):
+        onehot[slot] = (rows_ref[slot : slot + 1, :] == row_index).astype(jnp.bfloat16)
+
+    def wait_hidden(source, chunk):
+        hidden_copy(source, chunk, 0, across).wait_recv()
+
+    for distance in range(1, n // 2):
+        for chunk in range(CHUNKS):
+            for sign, onward, here, slot in (
+                (-1, has_upper, place_z - distance >= 0, 3 * distance),
+                (1, has_lower, place_z + distance <= last_z, 3 * distance + n),
+            ):
+                source = me + sign * 2 * distance
+                pl.when(here)(functools.partial(wait_hidden, source, chunk))
+                launch(
+                    hidden_copy(source, chunk, slot, me - sign * 2),
+                    jnp.logical_and(here, onward),
+                )
+                launch(hidden_copy(source, chunk, slot + 1, across), here)
+
+    for source in range(n // 2):
+        source = 2 * source + lax.rem(across, 2)
+        for chunk in range(CHUNKS):
+            wait_hidden(source, chunk)
+
     for step, other in enumerate(others()):
         launch(
             remote(
@@ -202,28 +272,8 @@
                 peer(other),
             )
         )
-    meta_in[me] = meta_out[me]
-
-    row_index = lax.broadcasted_iota(jnp.int32, (BLOCK, used), 0)
-    for slot in range(n):
-        onehot[slot] = (rows_ref[slot : slot + 1, :] == row_index).astype(jnp.bfloat16)
-
-    def wait_hidden(source):
-        remote(
-            held.at[source], held.at[source], hidden_send.at[0], hidden_recv.at[source], sibling
-        ).wait_recv()
-
-    for step, other in enumerate(line):
-        wait_hidden(other)
-        launch(
-            remote(
-                held.at[other],
-                held.at[other],
-                hidden_send.at[n // 2 + step],
-                hidden_recv.at[other],
-                peer(across),
-            )
-        )
+    weight_copy.wait()
+    own_copy.wait()
 
     place_index = lax.broadcasted_iota(jnp.int32, (BLOCK, used), 0).astype(jnp.float32)
 
@@ -235,19 +285,6 @@
                 place = meta[member : member + 1, :] - float(tile * BLOCK)
                 block = jnp.where(place == place_index, meta[4 + member : 5 + member, :], block)
             dense[source, tile * BLOCK : (tile + 1) * BLOCK, :] = block.astype(jnp.bfloat16)
-
-    for other in others():
-        remote(
-            meta_in.at[other], meta_in.at[other], meta_send.at[0], meta_recv.at[other], sibling
-        ).wait_recv()
-        build_dense(other)
-    build_dense(me)
-
-    weight_copy.wait()
-    own_copy.wait()
-    wait_hidden(across)
-    for other in line:
-        wait_hidden(other + across - me)
 
     def half_rows(which):
         blocks = held[pl.ds(which * half_blocks, half_blocks)]
@@ -329,6 +366,13 @@
             )
         )
     stats_in[me] = stats_out[...]
+
+    for other in others():
+        remote(
+            meta_in.at[other], meta_in.at[other], meta_send.at[0], meta_recv.at[other], sibling
+        ).wait_recv()
+        build_dense(other)
+    build_dense(me)
 
     for other in others():
         remote(
@@ -364,8 +408,11 @@
             block = block + factors[:, v : v + 1] * piece
         target_ref[:, cut] = block
 
-    for copy in sends:
-        copy.wait_send()
+    for copy, live in sends:
+        if live is None:
+            copy.wait_send()
+        else:
+            pl.when(live)(copy.wait_send)
 
 
 def fused(hidden_rows, head_weight, block_links, teacher_rows, offsets, link_weights):
@@ -383,16 +430,13 @@
             jax.ShapeDtypeStruct((1, tokens), jnp.float32),
             jax.ShapeDtypeStruct((tokens, columns), jnp.float32),
         ),
-        in_specs=[
-            pl.BlockSpec(memory_space=pl.ANY),
-            pl.BlockSpec(memory_space=pl.ANY),
-            pl.BlockSpec(memory_space=pltpu.SMEM),
-            vmem,
-            vmem,
-            vmem,
-        ],
+        in_specs=[pl.BlockSpec(memory_space=pl.ANY)] * 6,
         out_specs=(vmem, vmem),
         scratch_shapes=[
+            pltpu.SMEM(block_links.shape, jnp.int32),
+            pltpu.VMEM(teacher_rows.shape, jnp.int32),
+            pltpu.VMEM(offsets.shape, jnp.int32),
+            pltpu.VMEM(link_weights.shape, jnp.bfloat16),
             pltpu.VMEM((n, rows, depth), jnp.bfloat16),
             pltpu.VMEM((depth, columns), jnp.bfloat16),
             pltpu.VMEM((tokens, columns), jnp.float32),
@@ -407,9 +451,9 @@
             pltpu.VMEM((n, tokens, used), jnp.bfloat16),
             pltpu.VMEM((8, tokens), jnp.float32),
             pltpu.VMEM((n, 8, tokens), jnp.float32),
-            dma((2,)),
-            dma((n - 1,)),
-            dma((n,)),
+            dma((6,)),
+            dma((3 * n * CHUNKS,)),
+            dma((n * CHUNKS,)),
             dma((n - 1,)),
             dma((n,)),
             dma((tiles,)),
@@ -420,7 +464,7 @@
             dma((n,)),
         ],
         compiler_params=pltpu.CompilerParams(
-            collective_id=0, has_side_effects=True, vmem_limit_bytes=32 * 1024 * 1024
+            collective_id=0, has_side_effects=True, vmem_limit_bytes=60 * 1024 * 1024
         ),
     )(hidden_rows, head_weight, block_links, teacher_rows, offsets, link_weights)
     return log_partition.reshape(tokens), student_targets

time: 47 us -> 35.9 us (0.76)
  Pallas kernels: 39.2 us -> 32.2 us
  local copies, waits for them, and re-layouts: 6.82 us -> 2.89 us
    pallas_call x1, Pallas kernels: 39.2 us -> 32.2 us  [fused(): pl.pallas_call(functools.partial(fused_kernel, n), out_shape=(jax.ShapeDt...]
    unnamed x14 -> x2, local copies, waits for them, and re-layouts: 6.82 us -> 2.89 us
where the time goes in v2:
time: 35.9 us; the launch traced here: 35.7 us
  Pallas kernels  32.2 us (90%)
  local copies, waits for them, and re-layouts  2.89 us (8%)
  between operations  0.64 us (2%)
    pallas_call x1, Pallas kernels, fused(): pl.pallas_call(functools.partial(fused_kernel, n), out_shape=(jax.ShapeDt...  32.2 us
    unnamed x2, local copies, waits for them, and re-layouts  2.89 us

profile of v2, /device:TPU:0, one launch (start us, length us, event | category | flops | bytes accessed | tf_op | source)
XLA Modules:
  0.0 35.7 jit_solution(17504639607930449519)
XLA Ops:
  0.6 32.2 %shard_map.77 = (f32[1,128]{1,0:T(1,128)}, f32[128,768]{1,0:T(8,128)}) custom-call(bf16[32,2048]{1,0:T(8,128)(2,1)} %hidden_ref.1, bf16[2048,768]{1,0:T(8,128)(2,1)} %weight_ref.1, s32[2,8]{1,0:T(2,128)} %links_hbm.1, s32[8,128]{1,0:T(8,128)} %rows_hbm.1, s32[8,4,128]{2,1,0:T(4,128)} %offsets_hbm.1, bf16[8,4,128]{2,1,0:T(4,128)(2,1)} %link_weights_hbm.1), custom_call_target="tpu_custom_call" | custom-call | tf_op jit(solution)/shard_map/pallas_call | solution.py:427
  32.9 1.1 %copy.10 = f32[128]{0:T(128)} copy(f32[128]{0:T(128)} %bitcast.1) | data formatting | bytes 1024
  34.0 1.8 %copy.11 = f32[128,768]{1,0:T(8,128)} copy(f32[128,768]{1,0:T(8,128)} %get-tuple-element.9) | data formatting | bytes 786432

commit v3 on v2

--- a/solution.py
+++ b/solution.py
@@ -10,6 +10,7 @@
 
 BLOCK = 256
 CHUNKS = 2
+ORDER = (0, 1, -1, 2, -2, 3, -3)
 SB_DEV = 3
 
 
@@ -328,7 +329,7 @@
         exponents[tile] = exponent[:, tile * BLOCK : (tile + 1) * BLOCK].astype(jnp.bfloat16)
 
     running = jnp.zeros((tokens, used), jnp.float32)
-    for step, other in enumerate(others() + [me]):
+    for step, other in enumerate([lax.rem(me + n // 2 + k, n) for k in ORDER] + [me]):
         picked = jnp.dot(
             exponents[links_ref[0, other]], onehot[other], preferred_element_type=jnp.float32
         )

time: 35.9 us -> 35.4 us (0.986)
  Pallas kernels: 32.2 us -> 31.7 us
    pallas_call x1, Pallas kernels: 32.2 us -> 31.7 us  [fused(): pl.pallas_call(functools.partial(fused_kernel, n), out_shape=(jax.ShapeDt...]
where the time goes in v3:
time: 35.4 us; the launch traced here: 35.2 us
  Pallas kernels  31.7 us (90%)
  local copies, waits for them, and re-layouts  2.89 us (8%)
  between operations  0.64 us (2%)
    pallas_call x1, Pallas kernels, fused(): pl.pallas_call(functools.partial(fused_kernel, n), out_shape=(jax.ShapeDt...  31.7 us
    unnamed x2, local copies, waits for them, and re-layouts  2.89 us

profile of v3, /device:TPU:0, one launch (start us, length us, event | category | flops | bytes accessed | tf_op | source)
XLA Modules:
  0.0 35.2 jit_solution(12347898095828773885)
XLA Ops:
  0.6 31.7 %shard_map.77 = (f32[1,128]{1,0:T(1,128)}, f32[128,768]{1,0:T(8,128)}) custom-call(bf16[32,2048]{1,0:T(8,128)(2,1)} %hidden_ref.1, bf16[2048,768]{1,0:T(8,128)(2,1)} %weight_ref.1, s32[2,8]{1,0:T(2,128)} %links_hbm.1, s32[8,128]{1,0:T(8,128)} %rows_hbm.1, s32[8,4,128]{2,1,0:T(4,128)} %offsets_hbm.1, bf16[8,4,128]{2,1,0:T(4,128)(2,1)} %link_weights_hbm.1), custom_call_target="tpu_custom_call" | custom-call | tf_op jit(solution)/shard_map/pallas_call | solution.py:428
  32.4 1.1 %copy.10 = f32[128]{0:T(128)} copy(f32[128]{0:T(128)} %bitcast.1) | data formatting | bytes 1024
  33.5 1.8 %copy.11 = f32[128,768]{1,0:T(8,128)} copy(f32[128,768]{1,0:T(8,128)} %get-tuple-element.9) | data formatting | bytes 786432

commit v4 on v3

--- a/solution.py
+++ b/solution.py
@@ -263,6 +263,43 @@
         for chunk in range(CHUNKS):
             wait_hidden(source, chunk)
 
+    weight_copy.wait()
+    own_copy.wait()
+
+    place_index = lax.broadcasted_iota(jnp.int32, (BLOCK, used), 0).astype(jnp.float32)
+
+    def build_dense(source):
+        meta = meta_in[source]
+        for tile in range(tiles):
+            block = jnp.zeros((BLOCK, used), jnp.float32)
+            for member in range(4):
+                place = meta[member : member + 1, :] - float(tile * BLOCK)
+                block = jnp.where(place == place_index, meta[4 + member : 5 + member, :], block)
+            dense[source, tile * BLOCK : (tile + 1) * BLOCK, :] = block.astype(jnp.bfloat16)
+
+    def half_rows(which):
+        blocks = held[pl.ds(which * half_blocks, half_blocks)]
+        return blocks.reshape(tokens, blocks.shape[2])
+
+    for tile in range(tiles):
+        cut = slice(tile * BLOCK, (tile + 1) * BLOCK)
+        other_half[tile] = jnp.dot(
+            half_rows(1 - tok), weight[:, cut], preferred_element_type=jnp.float32
+        )
+        launch(
+            remote(
+                other_half.at[tile],
+                arrived_half.at[tile],
+                half_send.at[tile],
+                half_recv.at[tile],
+                sibling,
+            )
+        )
+    for tile in range(tiles):
+        cut = slice(tile * BLOCK, (tile + 1) * BLOCK)
+        own_half[:, cut] = jnp.dot(
+            half_rows(tok), weight[:, cut], preferred_element_type=jnp.float32
+        )
     for step, other in enumerate(others()):
         launch(
             remote(
@@ -272,43 +309,6 @@
                 meta_recv.at[me],
                 peer(other),
             )
-        )
-    weight_copy.wait()
-    own_copy.wait()
-
-    place_index = lax.broadcasted_iota(jnp.int32, (BLOCK, used), 0).astype(jnp.float32)
-
-    def build_dense(source):
-        meta = meta_in[source]
-        for tile in range(tiles):
-            block = jnp.zeros((BLOCK, used), jnp.float32)
-            for member in range(4):
-                place = meta[member : member + 1, :] - float(tile * BLOCK)
-                block = jnp.where(place == place_index, meta[4 + member : 5 + member, :], block)
-            dense[source, tile * BLOCK : (tile + 1) * BLOCK, :] = block.astype(jnp.bfloat16)
-
-    def half_rows(which):
-        blocks = held[pl.ds(which * half_blocks, half_blocks)]
-        return blocks.reshape(tokens, blocks.shape[2])
-
-    for tile in range(tiles):
-        cut = slice(tile * BLOCK, (tile + 1) * BLOCK)
-        other_half[tile] = jnp.dot(
-            half_rows(1 - tok), weight[:, cut], preferred_element_type=jnp.float32
-        )
-        launch(
-            remote(
-                other_half.at[tile],
-                arrived_half.at[tile],
-                half_send.at[tile],
-                half_recv.at[tile],
-                sibling,
-            )
-        )
-    for tile in range(tiles):
-        cut = slice(tile * BLOCK, (tile + 1) * BLOCK)
-        own_half[:, cut] = jnp.dot(
-            half_rows(tok), weight[:, cut], preferred_element_type=jnp.float32
         )
     for tile in range(tiles):
         cut = slice(tile * BLOCK, (tile + 1) * BLOCK)

time: 35.4 us -> 35.5 us (level)
  no operation moved by 1% of the time
where the time goes in v4:
time: 35.5 us; the launch traced here: 35.3 us
  Pallas kernels  31.8 us (90%)
  local copies, waits for them, and re-layouts  2.89 us (8%)
  between operations  0.64 us (2%)
    pallas_call x1, Pallas kernels, fused(): pl.pallas_call(functools.partial(fused_kernel, n), out_shape=(jax.ShapeDt...  31.8 us
    unnamed x2, local copies, waits for them, and re-layouts  2.89 us

profile of v4, /device:TPU:0, one launch (start us, length us, event | category | flops | bytes accessed | tf_op | source)
XLA Modules:
  0.0 35.3 jit_solution(3275020594771112474)
XLA Ops:
  0.6 31.8 %shard_map.77 = (f32[1,128]{1,0:T(1,128)}, f32[128,768]{1,0:T(8,128)}) custom-call(bf16[32,2048]{1,0:T(8,128)(2,1)} %hidden_ref.1, bf16[2048,768]{1,0:T(8,128)(2,1)} %weight_ref.1, s32[2,8]{1,0:T(2,128)} %links_hbm.1, s32[8,128]{1,0:T(8,128)} %rows_hbm.1, s32[8,4,128]{2,1,0:T(4,128)} %offsets_hbm.1, bf16[8,4,128]{2,1,0:T(4,128)(2,1)} %link_weights_hbm.1), custom_call_target="tpu_custom_call" | custom-call | tf_op jit(solution)/shard_map/pallas_call | solution.py:428
  32.4 1.1 %copy.10 = f32[128]{0:T(128)} copy(f32[128]{0:T(128)} %bitcast.1) | data formatting | bytes 1024
  33.6 1.8 %copy.11 = f32[128,768]{1,0:T(8,128)} copy(f32[128,768]{1,0:T(8,128)} %get-tuple-element.9) | data formatting | bytes 786432
